TPU v7x, 512 devices: a whole 4x4x16 slice. The times are simulated.
512 devices in a mesh: blk: 64 (over x, z_lo, core), head: 4 (over y), seq: 2 (over z_hi).
Axes of the slice: x: 4, y: 4, z: 16 (z_hi: 2, z_lo: 8; z = z_hi * 8 + z_lo), core: 2. Of those that a mesh axis runs over, the one named last changes fastest.
Arguments:
- query_rows: bfloat16 [16384, 2048], P(('seq', 'blk'), 'head'), parts along dimension 0, may hold values from -6 to 6
- key_rows: bfloat16 [16384, 2048], P(('seq', 'blk'), 'head'), parts along dimension 0, may hold values from -6 to 6
- value_rows: bfloat16 [16384, 2048], P(('seq', 'blk'), 'head'), parts along dimension 0, may hold values from -6 to 6
- kerple_power: float32 [16], P('head'), may hold values from 0.05 to 2
- kerple_scale: float32 [16], P('head'), may hold values from 0.1 to 4
- doc_lengths: int32 [8], P('seq'), parts along dimension 0, may hold values from 1 to 4096, 8192 in all
Outputs:
- attended: bfloat16 [16384, 2048], P(('seq', 'blk'), 'head'), parts along dimension 0
There are 2 independent parts, one for each index of `seq`. A program takes and returns all parts, laid end to end along the dimension named above; an argument that names none is the same for every part. Nothing has to cross between parts.
Inputs may be any that keep to these rules, and one draw needn't show every extreme that they name: `doc_lengths`: the lengths sum to 8192; the largest equals 4096.
All inputs are finite; a program needn't handle non-finite values.
Results may differ from a plain program's by a relative error of at most 0.0045.
Values may be sent and summed in bfloat16 or wider, within the bound.
A program may use at most 64 MiB of HBM per device.

v0:
```python
import functools
import math

import jax
import jax.numpy as jnp
from jax import lax
from jax.experimental import pallas as pl
from jax.experimental.pallas import tpu as pltpu
from jax.sharding import PartitionSpec as P

MESH = pl.DeviceIdType.MESH
NEG = -1e30
TINY = 1e-30
SIDE = 4
CELL = SIDE * SIDE
LOG2E = math.log2(math.e)
KEYS, VALUES, QUERIES = 0, 1, 2
EARLY, LATE = (KEYS, QUERIES), (VALUES,)


def kernel(
    rows,
    width,
    count,
    power_ref,
    scale_ref,
    lengths_ref,
    q_ref,
    k_ref,
    v_ref,
    out_ref,
    k_here,
    q_here,
    straight,
    turned,
    qcat,
    kcat,
    vbuf,
    shifts,
    acc,
    table,
    part_out,
    stat_out,
    part_in,
    stat_in,
    kept,
    merged,
    fetch_sem,
    deal_send,
    deal_recv,
    pass_send,
    pass_recv,
    share_send,
    share_recv,
    part_send,
    part_recv,
    stat_send,
    stat_recv,
    back_send,
    back_recv,
):
    me = lax.axis_index("blk")
    cell = me // CELL
    base = cell * CELL
    place = me - base
    head = place // SIDE
    mine = place % SIDE
    quarter = base + head * SIDE
    span = SIDE * rows

    barrier = pltpu.get_barrier_semaphore()
    fetch = pltpu.make_async_copy(v_ref, straight, fetch_sem.at[0])
    near_k = pltpu.make_async_copy(k_ref, k_here, fetch_sem.at[1])
    near_q = pltpu.make_async_copy(q_ref, q_here, fetch_sem.at[2])
    near_k.start()
    near_q.start()
    fetch.start()
    peers = 0
    up, down = me + CELL, me - CELL
    for n in range(SIDE):
        dealt_to, dealt_by, near = base + n * SIDE + head, base + mine * SIDE + n, quarter + n
        for other, meet in (
            (dealt_to, dealt_to != me),
            (dealt_by, (dealt_by != me) & (n != head)),
            (near, (near != me) & (mine != head) & (n != head)),
        ):
            peers = peers + meet.astype(jnp.int32)

            @pl.when(meet)
            def _():
                pl.semaphore_signal(barrier, inc=1, device_id={"blk": other}, device_id_type=MESH)

    for other, meet in (
        (up, up < count),
        (down, down >= 0),
        (up + CELL, up + CELL < count),
        (down - CELL, down >= CELL),
    ):
        peers = peers + meet.astype(jnp.int32)

        @pl.when(meet)
        def _():
            pl.semaphore_signal(barrier, inc=1, device_id={"blk": other}, device_id_type=MESH)

    near_k.wait()
    near_q.wait()
    pl.semaphore_wait(barrier, peers)

    own = pl.ds(pl.multiple_of(mine * rows, rows), rows)

    def deal(which, h):
        columns = pl.ds(h * width, width)
        src = (k_here.at[:, columns], turned.at[h], q_here.at[:, columns])[which]
        dst = (
            kcat.at[0, own, pl.ds(0, width)],
            vbuf.at[0, :, own],
            qcat.at[head, own, pl.ds(0, width)],
        )[which]
        return src, dst

    def start_deal(which, h):
        target = base + h * SIDE + head
        src, dst = deal(which, h)

        @pl.when(target != me)
        def _():
            pltpu.make_async_remote_copy(
                src_ref=src,
                dst_ref=dst,
                send_sem=deal_send.at[which, h],
                recv_sem=deal_recv.at[which, mine],
                device_id={"blk": target},
                device_id_type=MESH,
            ).start()

        @pl.when(target == me)
        def _():
            pltpu.make_async_copy(src, dst, deal_recv.at[which, mine]).start()

    def end_deal(which, h):
        src, _ = deal(which, h)

        @pl.when(base + h * SIDE + head != me)
        def _():
            pltpu.make_async_copy(src, src, deal_send.at[which, h]).wait()

    def turn_values():
        fetch.wait()
        for h in range(SIDE):
            block = straight[:, h * width : (h + 1) * width].astype(jnp.float32)
            turned[h] = block.T.astype(jnp.bfloat16)

    for which in EARLY:
        if which == VALUES:
            turn_values()
        for h in range(SIDE):
            start_deal(which, h)

    row_at = lax.broadcasted_iota(jnp.int32, (rows, rows), 0)
    col_at = lax.broadcasted_iota(jnp.int32, (rows, rows), 1)
    power = power_ref[head] * (-LOG2E)
    scale = scale_ref[head]

    def fill_table(at, _):
        distance = (at - (SIDE - 1)) * rows + col_at - row_at
        far = jnp.maximum(distance, 0).astype(jnp.float32)
        table[at] = jnp.where(distance >= 0, power * jnp.log(1.0 + scale * far), NEG)
        return 0

    lax.fori_loop(0, table.shape[0], fill_table, 0)

    ends = []
    for doc in range(lengths_ref.shape[0]):
        ends.append(lengths_ref[doc] + (ends[-1] if ends else 0))
    lane = lax.broadcasted_iota(jnp.int32, (rows, width), 1)
    line = lax.broadcasted_iota(jnp.int32, (rows, width), 0)

    def in_doc(start):
        position = line + start
        doc = jnp.zeros((rows, width), jnp.int32)
        for end in ends:
            doc = doc + (position >= end).astype(jnp.int32)
        return (doc == lane) & (position >= 0)

    def fill_query(at, _):
        group, part = at // SIDE, at % SIDE
        same = in_doc(base * rows + at * rows)
        where_to = pl.ds(pl.multiple_of(part * rows, rows), rows)
        qcat[group, where_to, pl.ds(width, width)] = jnp.where(same, 1.0, 0.0).astype(jnp.bfloat16)
        return 0

    def fill_key(at, _):
        back, part = at // SIDE, at % SIDE
        same = in_doc((base - back * CELL + mine * SIDE + part) * rows)
        fill = jnp.where(same | (lane >= len(ends)), 0.0, NEG).astype(jnp.bfloat16)
        where_to = pl.ds(pl.multiple_of(part * rows, rows), rows)
        kcat[back, where_to, pl.ds(width, width)] = fill
        return 0

    lax.fori_loop(0, CELL, fill_query, 0)
    lax.fori_loop(0, 3 * SIDE, fill_key, 0)

    def blank(back, _):
        kcat[back, :, pl.ds(0, width)] = jnp.zeros((span, width), jnp.bfloat16)
        vbuf[back] = jnp.zeros((width, span), jnp.bfloat16)
        return 0

    lax.fori_loop(jnp.minimum(cell + 1, 3), 3, blank, 0)
    for which in LATE:
        if which == VALUES:
            turn_values()
        for h in range(SIDE):
            start_deal(which, h)

    def held(which, back, slot):
        at = pl.ds(slot * rows, rows)
        return (kcat.at[back, at, pl.ds(0, width)], vbuf.at[back, :, at])[which]

    def dealt(which, slot):
        if which == QUERIES:
            block = qcat.at[mine, pl.ds(slot * rows, rows), pl.ds(0, width)]
        else:
            block = held(which, 0, slot)
        pltpu.make_async_copy(block, block, deal_recv.at[which, slot]).wait()

    def pass_on(which, back, slot):
        return pltpu.make_async_remote_copy(
            src_ref=held(which, 0, slot),
            dst_ref=held(which, back, slot),
            send_sem=pass_send.at[which, back - 1, slot],
            recv_sem=pass_recv.at[which, back - 1, slot],
            device_id={"blk": me + back * CELL},
            device_id_type=MESH,
        )

    def first_passes(which):
        for slot in range(SIDE):
            dealt(which, slot)
            for back in (1, 2):

                @pl.when(me + back * CELL < count)
                def _():
                    pass_on(which, back, slot).start()

    def passed(which):
        for back in (1, 2):

            @pl.when(cell >= back)
            def _():
                for slot in range(SIDE):
                    block = held(which, back, slot)
                    pltpu.make_async_copy(block, block, pass_recv.at[which, back - 1, slot]).wait()

    beside = mine + 1 - 2 * lax.rem(mine, 2)
    across = mine + 2 - 4 * (mine // 2)
    diagonal = SIDE - 1 - mine

    def share(group, to):
        block = qcat.at[group, :, pl.ds(0, width)]
        return pltpu.make_async_remote_copy(
            src_ref=block,
            dst_ref=block,
            send_sem=share_send.at[to],
            recv_sem=share_recv.at[group],
            device_id={"blk": quarter + to},
            device_id_type=MESH,
        )

    def shared(group):
        block = qcat.at[group, :, pl.ds(0, width)]
        pltpu.make_async_copy(block, block, share_recv.at[group]).wait()

    def share_own():
        for slot in range(SIDE):
            dealt(QUERIES, slot)
        share(mine, across).start()
        share(mine, beside).start()

    first_passes(KEYS)
    share_own()
    first_passes(VALUES)
    shared(across)
    hand_on = pltpu.make_async_remote_copy(
        src_ref=qcat.at[across, :, pl.ds(0, width)],
        dst_ref=qcat.at[across, :, pl.ds(0, width)],
        send_sem=share_send.at[diagonal],
        recv_sem=share_recv.at[across],
        device_id={"blk": quarter + beside},
        device_id_type=MESH,
    )
    hand_on.start()
    passed(KEYS)
    passed(VALUES)

    to_log2 = LOG2E / math.sqrt(width)

    def fold(combine, tile):
        return functools.reduce(combine, [tile[at : at + 8] for at in range(0, rows, 8)])

    def attend(first, pairs):
        group = mine if pairs == 3 else lax.rem(first + mine, SIDE)
        best = [jnp.full((8, rows), 2 * NEG, jnp.float32)] * SIDE
        for pair in range(pairs):
            m = first + pair * SIDE
            scores = lax.dot_general(
                kcat[(m + mine) // SIDE],
                qcat[group],
                (((1,), (1,)), ((), ())),
                preferred_element_type=jnp.float32,
            )
            for part in range(SIDE):
                for piece in range(SIDE):
                    shifted = (
                        scores[piece * rows : (piece + 1) * rows, part * rows : (part + 1) * rows]
                        * to_log2
                        + table[m * SIDE + part - piece + SIDE - 1]
                    )
                    shifts[pair, pl.ds(piece * rows, rows), pl.ds(part * rows, rows)] = shifted
                    best[part] = jnp.maximum(best[part], fold(jnp.maximum, shifted))
        tops = [jnp.max(tile, axis=0, keepdims=True) for tile in best]
        totals = [jnp.zeros((8, rows), jnp.float32)] * SIDE
        for pair in range(pairs):
            m = first + pair * SIDE
            probs = []
            for part in range(SIDE):
                weights = []
                for piece in range(SIDE):
                    shifted = shifts[pair, pl.ds(piece * rows, rows), pl.ds(part * rows, rows)]
                    weight = jnp.exp2(shifted - tops[part])
                    totals[part] = totals[part] + fold(jnp.add, weight)
                    weights.append(weight.astype(jnp.bfloat16))
                probs.append(jnp.concatenate(weights, axis=0))
            product = jnp.dot(
                vbuf[(m + mine) // SIDE],
                jnp.concatenate(probs, axis=1),
                preferred_element_type=jnp.float32,
            )
            acc[...] = product if pair == 0 else acc[...] + product
        for part in range(SIDE):
            total = jnp.sum(totals[part], axis=0, keepdims=True)
            level = tops[part] + jnp.log2(total)
            at = pl.ds(part * rows, rows)
            if pairs == 3:
                kept[:, at] = acc[:, at] / total
            else:
                part_out[group, :, at] = (acc[:, at] / total).astype(jnp.bfloat16)
            stat_out[group, pl.ds(part, 1), :] = level

    def hand_over(group):
        parts = [
            pltpu.make_async_remote_copy(
                src_ref=part_out.at[group, :, pl.ds(part * rows, rows)],
                dst_ref=part_in.at[mine, :, pl.ds(part * rows, rows)],
                send_sem=part_send.at[group, part],
                recv_sem=part_recv.at[mine, part],
                device_id={"blk": quarter + group},
                device_id_type=MESH,
            )
            for part in range(SIDE)
        ]
        stat = pltpu.make_async_remote_copy(
            src_ref=stat_out.at[group],
            dst_ref=stat_in.at[mine],
            send_sem=stat_send.at[group],
            recv_sem=stat_recv.at[mine],
            device_id={"blk": quarter + group},
            device_id_type=MESH,
        )
        return [stat] + parts

    def turn(group, _):
        @pl.when(group == mine)
        def _():
            attend(0, 3)

        @pl.when(group != mine)
        def _():
            @pl.when(group != across)
            def _():
                shared(group)

            attend(lax.rem(group - mine + SIDE, SIDE), 2)
            for copy in hand_over(group):
                copy.start()

        return 0

    lax.fori_loop(0, SIDE, turn, 0)

    others = [lax.rem(mine + step, SIDE) for step in range(1, SIDE)]
    for other in others:
        block = stat_in.at[other]
        pltpu.make_async_copy(block, block, stat_recv.at[other]).wait()

    def home(part):
        src = merged.at[pl.ds(part * rows, rows)]
        dst = out_ref.at[:, pl.ds(pl.multiple_of(head * width, width), width)]
        return src, dst, base + mine * SIDE + part

    def send_home(part):
        src, dst, target = home(part)
        return pltpu.make_async_remote_copy(
            src_ref=src,
            dst_ref=dst,
            send_sem=back_send.at[part],
            recv_sem=back_recv.at[head],
            device_id={"blk": target},
            device_id_type=MESH,
        )

    for part in range(SIDE):
        at = pl.ds(part * rows, rows)
        for other in others:
            block = part_in.at[other, :, at]
            pltpu.make_async_copy(block, block, part_recv.at[other, part]).wait()
        values = [kept[:, at]] + [part_in[other, :, at] for other in others]
        levels = [stat_out[mine, pl.ds(part, 1), :]]
        levels += [stat_in[other, pl.ds(part, 1), :] for other in others]
        most = functools.reduce(jnp.maximum, levels)
        shares = [jnp.exp2(level - most) for level in levels]
        total = functools.reduce(jnp.add, shares)
        whole = [v.astype(jnp.float32) * s for v, s in zip(values, shares)]
        whole = functools.reduce(jnp.add, whole) / total
        merged[at, :] = whole.T.astype(jnp.bfloat16)
        src, dst, target = home(part)

        @pl.when(target != me)
        def _():
            send_home(part).start()

        @pl.when(target == me)
        def _():
            pltpu.make_async_copy(src, dst, back_recv.at[head]).start()

    for h in range(SIDE):
        block = out_ref.at[:, pl.ds(h * width, width)]
        pltpu.make_async_copy(block, block, back_recv.at[h]).wait()

    for which in range(3):
        for h in range(SIDE):
            end_deal(which, h)
    share(mine, across).wait_send()
    share(mine, beside).wait_send()
    hand_on.wait_send()
    for which in (KEYS, VALUES):
        for back in (1, 2):

            @pl.when(me + back * CELL < count)
            def _():
                for slot in range(SIDE):
                    pass_on(which, back, slot).wait_send()

    for other in others:
        for copy in hand_over(other):
            copy.wait_send()
    for part in range(SIDE):

        @pl.when(base + mine * SIDE + part != me)
        def _():
            send_home(part).wait_send()


def on_device(query_rows, key_rows, value_rows, kerple_power, kerple_scale, doc_lengths):
    count = lax.axis_size("blk")
    rows, columns = query_rows.shape
    width = columns // SIDE
    span = SIDE * rows
    return pl.pallas_call(
        functools.partial(kernel, rows, width, count),
        out_shape=pltpu.VMEM((rows, columns), jnp.bfloat16),
        in_specs=[pl.BlockSpec(memory_space=pltpu.SMEM)] * 3 + [pl.BlockSpec(memory_space=pl.ANY)] * 3,
        out_specs=pl.BlockSpec(memory_space=pltpu.VMEM),
        scratch_shapes=[
            pltpu.VMEM((rows, columns), jnp.bfloat16),
            pltpu.VMEM((rows, columns), jnp.bfloat16),
            pltpu.VMEM((rows, columns), jnp.bfloat16),
            pltpu.VMEM((SIDE, width, rows), jnp.bfloat16),
            pltpu.VMEM((SIDE, span, 2 * width), jnp.bfloat16),
            pltpu.VMEM((3, span, 2 * width), jnp.bfloat16),
            pltpu.VMEM((3, width, span), jnp.bfloat16),
            pltpu.VMEM((3, span, span), jnp.float32),
            pltpu.VMEM((width, span), jnp.float32),
            pltpu.VMEM((2 * CELL + 2 * SIDE - 1, rows, rows), jnp.float32),
            pltpu.VMEM((SIDE, width, span), jnp.bfloat16),
            pltpu.VMEM((SIDE, 2 * SIDE, rows), jnp.float32),
            pltpu.VMEM((SIDE, width, span), jnp.bfloat16),
            pltpu.VMEM((SIDE, 2 * SIDE, rows), jnp.float32),
            pltpu.VMEM((width, span), jnp.float32),
            pltpu.VMEM((span, width), jnp.bfloat16),
            pltpu.SemaphoreType.DMA((3,)),
            pltpu.SemaphoreType.DMA((3, SIDE)),
            pltpu.SemaphoreType.DMA((3, SIDE)),
            pltpu.SemaphoreType.DMA((2, 2, SIDE)),
            pltpu.SemaphoreType.DMA((2, 2, SIDE)),
            pltpu.SemaphoreType.DMA((SIDE,)),
            pltpu.SemaphoreType.DMA((SIDE,)),
            pltpu.SemaphoreType.DMA((SIDE, SIDE)),
            pltpu.SemaphoreType.DMA((SIDE, SIDE)),
            pltpu.SemaphoreType.DMA((SIDE,)),
            pltpu.SemaphoreType.DMA((SIDE,)),
            pltpu.SemaphoreType.DMA((SIDE,)),
            pltpu.SemaphoreType.DMA((SIDE,)),
        ],
        compiler_params=pltpu.CompilerParams(
            collective_id=0, has_side_effects=True, vmem_limit_bytes=60 * 2**20
        ),
    )(kerple_power, kerple_scale, doc_lengths, query_rows, key_rows, value_rows)


def solution(mesh):
    block = P(("seq", "blk"), "head")
    return jax.shard_map(
        on_device,
        mesh=mesh,
        in_specs=(block, block, block, P("head"), P("head"), P("seq")),
        out_specs=block,
        check_vma=False,
    )
```

profile of v0, /device:TPU:109, one launch (start us, length us, event | category | flops | bytes accessed | tf_op | source)
XLA Modules:
  0.0 47.7 jit_solution(9497469376668025131)
XLA Ops:
  0.0 47.1 %shard_map.64 = bf16[128,512]{1,0:T(8,128)(2,1)S(1)} custom-call(f32[4]{0:T(128)} %power_ref.1, f32[4]{0:T(128)} %scale_ref.1, s32[4]{0:T(128)} %lengths_ref.1, bf16[128,512]{1,0:T(8,128)(2,1)} %q_ref.1, bf16[128,512]{1,0:T(8,128)(2,1)} %k_ref.1, bf16[128,512]{1,0:T(8,128)(2,1)} %v_ref.1), custom_call_target="tpu_custom_call" | custom-call | tf_op jit(solution)/shard_map/pallas_call | solution.py:468
  47.1 0.7 %copy.8 = bf16[128,512]{1,0:T(8,128)(2,1)} copy(bf16[128,512]{1,0:T(8,128)(2,1)S(1)} %shard_map.64) | data formatting | bytes 262144
where the time goes:
time: 47.9 us; the launch traced here: 47.7 us
  Pallas kernels  47.1 us (98%)
  local copies, waits for them, and re-layouts  0.66 us (1%)
    pallas_call x1, Pallas kernels, on_device(): pl.pallas_call(functools.partial(kernel, rows, width, count), out_shape=p...  47.1 us

commit v1 on v0

--- a/solution.py
+++ b/solution.py
@@ -242,11 +242,10 @@
                 def _():
                     pass_on(which, back, slot).start()
 
-    def passed(which):
-        for back in (1, 2):
-
-            @pl.when(cell >= back)
-            def _():
+    def passed(back):
+        @pl.when(cell >= back)
+        def _():
+            for which in (KEYS, VALUES):
                 for slot in range(SIDE):
                     block = held(which, back, slot)
                     pltpu.make_async_copy(block, block, pass_recv.at[which, back - 1, slot]).wait()
@@ -289,8 +288,7 @@
         device_id_type=MESH,
     )
     hand_on.start()
-    passed(KEYS)
-    passed(VALUES)
+    passed(1)
 
     to_log2 = LOG2E / math.sqrt(width)
 
@@ -368,24 +366,29 @@
         )
         return [stat] + parts
 
-    def turn(group, _):
-        @pl.when(group == mine)
-        def _():
-            attend(0, 3)
-
-        @pl.when(group != mine)
-        def _():
-            @pl.when(group != across)
-            def _():
-                shared(group)
-
-            attend(lax.rem(group - mine + SIDE, SIDE), 2)
-            for copy in hand_over(group):
-                copy.start()
-
+    def turn(order, _):
+        group = order + (order >= mine).astype(jnp.int32)
+
+        @pl.when(group != across)
+        def _():
+            shared(group)
+
+        attend(lax.rem(group - mine + SIDE, SIDE), 2)
+        for copy in hand_over(group):
+            copy.start()
         return 0
 
-    lax.fori_loop(0, SIDE, turn, 0)
+    @pl.when(mine > 0)
+    def _():
+        passed(2)
+
+    lax.fori_loop(0, SIDE - 1, turn, 0)
+
+    @pl.when(mine == 0)
+    def _():
+        passed(2)
+
+    attend(0, 3)
 
     others = [lax.rem(mine + step, SIDE) for step in range(1, SIDE)]
     for other in others:

time: 47.9 us -> 47.8 us (level)
  no operation moved by 1% of the time
where the time goes in v1:
time: 47.8 us; the launch traced here: 47.6 us
  Pallas kernels  46.9 us (98%)
  local copies, waits for them, and re-layouts  0.66 us (1%)
    pallas_call x1, Pallas kernels, on_device(): pl.pallas_call(functools.partial(kernel, rows, width, count), out_shape=p...  46.9 us

profile of v1, /device:TPU:109, one launch (start us, length us, event | category | flops | bytes accessed | tf_op | source)
XLA Modules:
  0.0 47.6 jit_solution(8273727445148886861)
XLA Ops:
  0.0 46.9 %shard_map.64 = bf16[128,512]{1,0:T(8,128)(2,1)S(1)} custom-call(f32[4]{0:T(128)} %power_ref.1, f32[4]{0:T(128)} %scale_ref.1, s32[4]{0:T(128)} %lengths_ref.1, bf16[128,512]{1,0:T(8,128)(2,1)} %q_ref.1, bf16[128,512]{1,0:T(8,128)(2,1)} %k_ref.1, bf16[128,512]{1,0:T(8,128)(2,1)} %v_ref.1), custom_call_target="tpu_custom_call" | custom-call | tf_op jit(solution)/shard_map/pallas_call | solution.py:471
  46.9 0.7 %copy.8 = bf16[128,512]{1,0:T(8,128)(2,1)} copy(bf16[128,512]{1,0:T(8,128)(2,1)S(1)} %shard_map.64) | data formatting | bytes 262144

commit v2 on v1

--- a/solution.py
+++ b/solution.py
@@ -242,13 +242,12 @@
                 def _():
                     pass_on(which, back, slot).start()
 
-    def passed(back):
-        @pl.when(cell >= back)
-        def _():
-            for which in (KEYS, VALUES):
-                for slot in range(SIDE):
-                    block = held(which, back, slot)
-                    pltpu.make_async_copy(block, block, pass_recv.at[which, back - 1, slot]).wait()
+    def passed(which, back, needed):
+        @pl.when((cell >= back) & needed)
+        def _():
+            for slot in range(SIDE):
+                block = held(which, back, slot)
+                pltpu.make_async_copy(block, block, pass_recv.at[which, back - 1, slot]).wait()
 
     beside = mine + 1 - 2 * lax.rem(mine, 2)
     across = mine + 2 - 4 * (mine // 2)
@@ -288,14 +287,15 @@
         device_id_type=MESH,
     )
     hand_on.start()
-    passed(1)
+    passed(KEYS, 1, True)
+    passed(KEYS, 2, mine > 0)
 
     to_log2 = LOG2E / math.sqrt(width)
 
     def fold(combine, tile):
         return functools.reduce(combine, [tile[at : at + 8] for at in range(0, rows, 8)])
 
-    def attend(first, pairs):
+    def attend(first, pairs, await_values):
         group = mine if pairs == 3 else lax.rem(first + mine, SIDE)
         best = [jnp.full((8, rows), 2 * NEG, jnp.float32)] * SIDE
         for pair in range(pairs):
@@ -316,6 +316,7 @@
                     shifts[pair, pl.ds(piece * rows, rows), pl.ds(part * rows, rows)] = shifted
                     best[part] = jnp.maximum(best[part], fold(jnp.maximum, shifted))
         tops = [jnp.max(tile, axis=0, keepdims=True) for tile in best]
+        await_values()
         totals = [jnp.zeros((8, rows), jnp.float32)] * SIDE
         for pair in range(pairs):
             m = first + pair * SIDE
@@ -373,22 +374,19 @@
         def _():
             shared(group)
 
-        attend(lax.rem(group - mine + SIDE, SIDE), 2)
+        def await_values():
+            passed(VALUES, 1, order == 0)
+            passed(VALUES, 2, (order == 0) & (mine > 0))
+
+        attend(lax.rem(group - mine + SIDE, SIDE), 2, await_values)
         for copy in hand_over(group):
             copy.start()
         return 0
 
-    @pl.when(mine > 0)
-    def _():
-        passed(2)
-
     lax.fori_loop(0, SIDE - 1, turn, 0)
 
-    @pl.when(mine == 0)
-    def _():
-        passed(2)
-
-    attend(0, 3)
+    passed(KEYS, 2, mine == 0)
+    attend(0, 3, lambda: passed(VALUES, 2, mine == 0))
 
     others = [lax.rem(mine + step, SIDE) for step in range(1, SIDE)]
     for other in others:

time: 47.8 us -> 47.4 us (level)
  the two profiles are of different devices: /device:TPU:109 before, /device:TPU:125 now
where the time goes in v2:
time: 47.4 us; the launch traced here: 47.2 us
  Pallas kernels  46.6 us (98%)
  local copies, waits for them, and re-layouts  0.66 us (1%)
    pallas_call x1, Pallas kernels, on_device(): pl.pallas_call(functools.partial(kernel, rows, width, count), out_shape=p...  46.6 us

profile of v2, /device:TPU:125, one launch (start us, length us, event | category | flops | bytes accessed | tf_op | source)
XLA Modules:
  0.0 47.2 jit_solution(11485873940431443911)
XLA Ops:
  0.0 46.6 %shard_map.64 = bf16[128,512]{1,0:T(8,128)(2,1)S(1)} custom-call(f32[4]{0:T(128)} %power_ref.1, f32[4]{0:T(128)} %scale_ref.1, s32[4]{0:T(128)} %lengths_ref.1, bf16[128,512]{1,0:T(8,128)(2,1)} %q_ref.1, bf16[128,512]{1,0:T(8,128)(2,1)} %k_ref.1, bf16[128,512]{1,0:T(8,128)(2,1)} %v_ref.1), custom_call_target="tpu_custom_call" | custom-call | tf_op jit(solution)/shard_map/pallas_call | solution.py:469
  46.6 0.7 %copy.8 = bf16[128,512]{1,0:T(8,128)(2,1)} copy(bf16[128,512]{1,0:T(8,128)(2,1)S(1)} %shard_map.64) | data formatting | bytes 262144

commit v3 on v2

--- a/solution.py
+++ b/solution.py
@@ -316,10 +316,9 @@
                     shifts[pair, pl.ds(piece * rows, rows), pl.ds(part * rows, rows)] = shifted
                     best[part] = jnp.maximum(best[part], fold(jnp.maximum, shifted))
         tops = [jnp.max(tile, axis=0, keepdims=True) for tile in best]
-        await_values()
         totals = [jnp.zeros((8, rows), jnp.float32)] * SIDE
+        weighed = []
         for pair in range(pairs):
-            m = first + pair * SIDE
             probs = []
             for part in range(SIDE):
                 weights = []
@@ -329,9 +328,13 @@
                     totals[part] = totals[part] + fold(jnp.add, weight)
                     weights.append(weight.astype(jnp.bfloat16))
                 probs.append(jnp.concatenate(weights, axis=0))
+            weighed.append(jnp.concatenate(probs, axis=1))
+        await_values()
+        for pair in range(pairs):
+            m = first + pair * SIDE
             product = jnp.dot(
                 vbuf[(m + mine) // SIDE],
-                jnp.concatenate(probs, axis=1),
+                weighed[pair],
                 preferred_element_type=jnp.float32,
             )
             acc[...] = product if pair == 0 else acc[...] + product

time: 47.4 us -> 47.7 us (level)
  the two profiles are of different devices: /device:TPU:125 before, /device:TPU:109 now
where the time goes in v3:
time: 47.7 us; the launch traced here: 47.6 us
  Pallas kernels  46.9 us (98%)
  local copies, waits for them, and re-layouts  0.66 us (1%)
    pallas_call x1, Pallas kernels, on_device(): pl.pallas_call(functools.partial(kernel, rows, width, count), out_shape=p...  46.9 us

profile of v3, /device:TPU:109, one launch (start us, length us, event | category | flops | bytes accessed | tf_op | source)
XLA Modules:
  0.0 47.6 jit_solution(7188706105537833787)
XLA Ops:
  0.0 46.9 %shard_map.64 = bf16[128,512]{1,0:T(8,128)(2,1)S(1)} custom-call(f32[4]{0:T(128)} %power_ref.1, f32[4]{0:T(128)} %scale_ref.1, s32[4]{0:T(128)} %lengths_ref.1, bf16[128,512]{1,0:T(8,128)(2,1)} %q_ref.1, bf16[128,512]{1,0:T(8,128)(2,1)} %k_ref.1, bf16[128,512]{1,0:T(8,128)(2,1)} %v_ref.1), custom_call_target="tpu_custom_call" | custom-call | tf_op jit(solution)/shard_map/pallas_call | solution.py:472
  46.9 0.7 %copy.8 = bf16[128,512]{1,0:T(8,128)(2,1)} copy(bf16[128,512]{1,0:T(8,128)(2,1)S(1)} %shard_map.64) | data formatting | bytes 262144
